TPU v7x, 256 devices: a whole 4x4x8 slice. The times are simulated.
256 devices in a mesh: tm: 8 (over x, core), rows: 32 (over y, z).
Axes of the slice: x: 4, y: 4, z: 8, core: 2. Of those that a mesh axis runs over, the one named last changes fastest.
Arguments:
- frames: bfloat16 [16, 32, 160, 384], P('tm', 'rows'), may hold values from -6 to 6
- first_cache: bfloat16 [2, 32, 160, 384], P(None, 'rows'), may hold values from -6 to 6
- second_cache: bfloat16 [2, 32, 160, 384], P(None, 'rows'), may hold values from -6 to 6
- first_gain: float32 [384], replicated, may hold values from 0.1 to 1.9
- second_gain: float32 [384], replicated, may hold values from 0.1 to 1.9
- first_weight: bfloat16 [3, 3, 3, 384, 384], P(None, None, None, None, 'rows'), may hold values from -0.0625 to 0.0625
- second_weight: bfloat16 [3, 3, 3, 384, 384], P(None, None, None, None, 'rows'), may hold values from -0.0625 to 0.0625
- upsample_weight: bfloat16 [3, 3, 384, 192], replicated, may hold values from -0.109375 to 0.109375
Outputs:
- upsampled: bfloat16 [16, 64, 320, 192], P('tm', 'rows')
All inputs are finite; a program needn't handle non-finite values.
Results may differ from a plain program's by a relative error of at most 0.015.
Values may be sent and summed in bfloat16 or wider, within the bound.
A program may use at most 128 MiB of HBM per device.

v0:
```python
import jax
import jax.numpy as jnp
from jax import lax
from jax.sharding import PartitionSpec as P


def shifted(block, axis, distance):
    devices = range(lax.axis_size(axis))
    route = [(i - distance, i) for i in devices if i - distance in devices]
    return lax.ppermute(block, axis, route)


def extended(block, sides, width):
    for axis, dim in sides:
        count = lax.axis_size(axis)
        forward = [(i, i + 1) for i in range(count - 1)]
        backward = [(target, source) for source, target in forward]
        low = lax.ppermute(
            lax.slice_in_dim(block, block.shape[dim] - width, None, axis=dim), axis, forward
        )
        high = lax.ppermute(lax.slice_in_dim(block, 0, width, axis=dim), axis, backward)
        block = jnp.concatenate([low, block, high], axis=dim)
    return block


def channel_norm(values, gain):
    values = values.astype(jnp.float32)
    scale = lax.rsqrt(jnp.mean(values * values, axis=-1, keepdims=True) + 1e-06)
    return values * scale * gain


def tap_expand(padded):
    height = padded.shape[1] - 2
    width = padded.shape[2]
    spread = jnp.pad(padded, ((0, 0), (0, 0), (1, 1), (0, 0)))
    pieces = []
    for row_tap in range(3):
        for col_tap in range(3):
            pieces.append(spread[:, row_tap : row_tap + height, col_tap : col_tap + width])
    return jnp.concatenate(pieces, axis=-1)


def conv_taps(padded, weight):
    count = padded.shape[0] - 2
    height = padded.shape[1] - 2
    width = padded.shape[2]
    outputs = weight.shape[-1]
    expanded = tap_expand(padded)
    depth = expanded.shape[-1]
    total = jnp.zeros((count * height * width, outputs), jnp.float32)
    for time_tap in range(3):
        block = expanded[time_tap : time_tap + count].reshape(-1, depth)
        total = total + jnp.dot(
            block, weight[time_tap].reshape(depth, outputs), preferred_element_type=jnp.float32
        )
    return total.reshape(count, height, width, outputs)


def shards(
    frames,
    first_cache,
    second_cache,
    first_gain,
    second_gain,
    first_weight,
    second_weight,
    upsample_weight,
):
    group = lax.axis_index("tm")
    first_input = jax.nn.silu(channel_norm(frames, first_gain)).astype(jnp.bfloat16)
    prior = shifted(first_input, "tm", 1)
    prior = jnp.where(group == 0, first_cache, prior)
    joined = jnp.concatenate([prior, first_input], axis=0)
    padded_first = extended(joined, (("rows", 1),), 1)
    first_out = conv_taps(padded_first, lax.all_gather(first_weight, "rows", axis=4, tiled=True))
    first_out = first_out.astype(jnp.bfloat16)
    second_input = jax.nn.silu(channel_norm(first_out, second_gain)).astype(jnp.bfloat16)
    before = shifted(second_input, "tm", 1)
    before = jnp.where(group == 0, second_cache, before)
    joined_second = jnp.concatenate([before, second_input], axis=0)
    padded_second = extended(joined_second, (("rows", 1),), 1)
    second_out = conv_taps(padded_second, lax.all_gather(second_weight, "rows", axis=4, tiled=True))
    block_out = (frames.astype(jnp.float32) + second_out).astype(jnp.bfloat16)
    bordered = extended(block_out, (("rows", 1),), 1)
    taller = jnp.repeat(bordered, 2, axis=1)[:, 1:-1]
    larger = jnp.repeat(taller, 2, axis=2)
    count = larger.shape[0]
    height = larger.shape[1] - 2
    width = larger.shape[2]
    outputs = upsample_weight.shape[-1]
    expanded = tap_expand(larger)
    depth = expanded.shape[-1]
    total = jnp.dot(
        expanded.reshape(-1, depth),
        upsample_weight.reshape(depth, outputs),
        preferred_element_type=jnp.float32,
    )
    return total.reshape(count, height, width, outputs).astype(jnp.bfloat16)


def solution(mesh):
    in_specs = (
        P("tm", "rows", None, None),
        P(None, "rows", None, None),
        P(None, "rows", None, None),
        P(),
        P(),
        P(None, None, None, None, "rows"),
        P(None, None, None, None, "rows"),
        P(),
    )
    out_specs = P("tm", "rows", None, None)
    return jax.shard_map(shards, mesh=mesh, in_specs=in_specs, out_specs=out_specs, check_vma=False)
```

profile of v0, /device:TPU:10, one launch (start us, length us, event | category | flops | bytes accessed | tf_op | source)
XLA Modules:
  0.0 317.1 jit_solution(2051383408447645561)
XLA Ops:
  6.5 1.8 copy.16
  8.4 1.8 copy.21
  10.3 1.1 fusion.18
  11.4 1.2 fusion.25
  12.6 1.9 collective-permute-start
  14.5 5.6 %collective-permute-done = bf16[2,1,160,384]{3,2,1,0:T(8,128)(2,1)S(1)} collective-permute-done((bf16[2,1,160,384]{3,2,1,0:T(8,128)(2,1)S(1)}, bf16[2,1,160,384]{3,2,1,0:T(8,128)(2,1)S(1)}, u32[]{:S(2)}, u32[]{:S(2)}) %collective-permute-start) | collective-permute-done | bytes 245792 | tf_op jit(solution)/shard_map/ppermute | solution.py:10
  20.2 3.8 %collective-permute-start.1 = (bf16[4,1,160,384]{3,2,1,0:T(8,128)(2,1)S(1)}, bf16[4,1,160,384]{3,2,1,0:T(8,128)(2,1)S(1)}, u32[]{:S(2)}, u32[]{:S(2)}) collective-permute-start(bf16[4,1,160,384]{3,2,1,0:T(8,128)(2,1)S(1)} %pad_maximum_fusion.1), channel_id=1, source_target_pairs={{0,1},{1,2},{2,3},{3,4},{4,5},{5,6},{6,7},{7,8},{8,9},{9,10},{10,1... | collective-permute-start | bytes 1474568 | tf_op jit(solution)/shard_map/ppermute | solution.py:18
  24.0 5.7 %collective-permute-start.2 = (bf16[4,1,160,384]{3,2,1,0:T(8,128)(2,1)S(1)}, bf16[4,1,160,384]{3,2,1,0:T(8,128)(2,1)S(1)}, u32[]{:S(2)}, u32[]{:S(2)}) collective-permute-start(bf16[4,1,160,384]{3,2,1,0:T(8,128)(2,1)S(1)} %pad_maximum_fusion.1), channel_id=1, source_target_pairs={{1,0},{2,1},{3,2},{4,3},{5,4},{6,5},{7,6},{8,7},{9,8},{10,9},{11,1... | collective-permute-start | bytes 1474568 | tf_op jit(solution)/shard_map/ppermute | solution.py:21
  29.8 15.7 %collective-permute-done.1 = bf16[4,1,160,384]{3,2,1,0:T(8,128)(2,1)S(1)} collective-permute-done((bf16[4,1,160,384]{3,2,1,0:T(8,128)(2,1)S(1)}, bf16[4,1,160,384]{3,2,1,0:T(8,128)(2,1)S(1)}, u32[]{:S(2)}, u32[]{:S(2)}) %collective-permute-start.1) | collective-permute-done | bytes 491552 | tf_op jit(solution)/shard_map/ppermute | solution.py:18
  45.5 1.0 collective-permute-done.2
  46.5 0.5 fusion.8
  48.0 2.9 fusion.30
  50.9 72.1 %all-gather.3.cloned.1.call-done = bf16[3,3,3,384,384]{3,2,1,0,4:T(4,128)(2,1)} async-done(((bf16[3,3,3,384,12]{3,2,1,0,4:T(4,128)(2,1)}), bf16[3,3,3,384,384]{3,2,1,0,4:T(4,128)(2,1)}) %all-gather.3.cloned.1.call-update) | async-done | bytes 7962640 | tf_op jit(solution)/shard_map/all_gather | solution.py:75
  123.0 8.7 %fusion.28 = (bf16[1,3,3,384,384]{3,2,1,0,4:T(4,128)(2,1)S(1)}, bf16[1,3,3,384,384]{3,2,1,0,4:T(4,128)(2,1)}, bf16[1,3,3,384,384]{3,2,1,0,4:T(4,128)(2,1)}) fusion(bf16[3,3,3,384,384]{3,2,1,0,4:T(4,128)(2,1)} %all-gather.3.cloned.1.call-done), kind=kLoop, calls=%fused_computation.73 | loop fusion | bytes 15925248 | tf_op jit(solution)/shard_map/slice | solution.py:54
  131.7 7.4 %copy.29 = bf16[1,3,3,384,384]{4,3,2,1,0:T(8,128)(2,1)} copy(bf16[1,3,3,384,384]{3,2,1,0,4:T(4,128)(2,1)} %get-tuple-element.9) | data formatting | bytes 5308416
  139.1 7.3 %copy.28 = bf16[1,3,3,384,384]{4,3,2,1,0:T(8,128)(2,1)} copy(bf16[1,3,3,384,384]{3,2,1,0,4:T(4,128)(2,1)} %get-tuple-element.10) | data formatting | bytes 5308416
  146.4 5.4 %copy.30 = bf16[1,3,3,384,384]{4,3,2,1,0:T(8,128)(2,1)} copy(bf16[1,3,3,384,384]{3,2,1,0,4:T(4,128)(2,1)S(1)} %get-tuple-element.8) | data formatting | bytes 5308416
  151.9 3.9 %fusion.31 = f32[320,384]{1,0:T(8,128)S(1)} fusion(bf16[320,3456]{1,0:T(8,128)(2,1)} %bitcast.48, bf16[3456,384]{1,0:T(8,128)(2,1)} %bitcast.45), kind=kOutput, calls=%fused_computation.76 | convolution fusion | flops 849346560 | bytes 5357568 | tf_op jit(solution)/shard_map/dot_general | solution.py:53
  155.8 1.3 convolution_add_fusion.3
  157.5 0.7 copy-done.9
  158.2 1.4 multiply_reduce_fusion
  160.0 1.9 collective-permute-start.3
  162.0 5.6 %collective-permute-done.3 = bf16[2,1,160,384]{3,2,1,0:T(8,128)(2,1)S(1)} collective-permute-done((bf16[2,1,160,384]{3,2,1,0:T(8,128)(2,1)S(1)}, bf16[2,1,160,384]{3,2,1,0:T(8,128)(2,1)S(1)}, u32[]{:S(2)}, u32[]{:S(2)}) %collective-permute-start.3) | collective-permute-done | bytes 245792 | tf_op jit(solution)/shard_map/ppermute | solution.py:10
  167.6 0.8 pad_maximum_fusion.2
  168.5 1.9 collective-permute-start.4
  170.4 6.2 %collective-permute-start.5 = (bf16[4,1,160,384]{3,2,1,0:T(8,128)(2,1)}, bf16[4,1,160,384]{3,2,1,0:T(8,128)(2,1)}, u32[]{:S(2)}, u32[]{:S(2)}) collective-permute-start(bf16[4,1,160,384]{3,2,1,0:T(8,128)(2,1)} %pad_maximum_fusion.2), channel_id=1, source_target_pairs={{1,0},{2,1},{3,2},{4,3},{5,4},{6,5},{7,6},{8,7},{9,8},{10,9},{11,1... | collective-permute-start | bytes 1474568 | tf_op jit(solution)/shard_map/ppermute | solution.py:21
  176.6 66.0 %all-gather.5.cloned.1.call-done = bf16[3,3,3,384,384]{3,2,1,0,4:T(4,128)(2,1)} async-done(((bf16[3,3,3,384,12]{3,2,1,0,4:T(4,128)(2,1)}), bf16[3,3,3,384,384]{3,2,1,0,4:T(4,128)(2,1)}) %all-gather.5.cloned.1.call-update) | async-done | bytes 7962640 | tf_op jit(solution)/shard_map/all_gather | solution.py:82
  242.6 8.7 %fusion.27 = (bf16[1,3,3,384,384]{3,2,1,0,4:T(4,128)(2,1)S(1)}, bf16[1,3,3,384,384]{3,2,1,0,4:T(4,128)(2,1)}, bf16[1,3,3,384,384]{3,2,1,0,4:T(4,128)(2,1)}) fusion(bf16[3,3,3,384,384]{3,2,1,0,4:T(4,128)(2,1)} %all-gather.5.cloned.1.call-done), kind=kLoop, calls=%fused_computation.72 | loop fusion | bytes 15925248 | tf_op jit(solution)/shard_map/slice | solution.py:54
  251.4 7.3 %copy.32 = bf16[1,3,3,384,384]{4,3,2,1,0:T(8,128)(2,1)} copy(bf16[1,3,3,384,384]{3,2,1,0,4:T(4,128)(2,1)} %get-tuple-element.6) | data formatting | bytes 5308416
  258.7 7.3 %copy.31 = bf16[1,3,3,384,384]{4,3,2,1,0:T(8,128)(2,1)} copy(bf16[1,3,3,384,384]{3,2,1,0,4:T(4,128)(2,1)} %get-tuple-element.7) | data formatting | bytes 5308416
  266.0 5.4 %copy.33 = bf16[1,3,3,384,384]{4,3,2,1,0:T(8,128)(2,1)} copy(bf16[1,3,3,384,384]{3,2,1,0,4:T(4,128)(2,1)S(1)} %get-tuple-element.5) | data formatting | bytes 5308416
  271.5 1.8 select_maximum_fusion
  273.3 1.1 constant_dynamic-update-slice_fusion.5
  275.1 1.1 constant_dynamic-update-slice_fusion.3
  276.8 1.3 copy-done.6
  278.1 1.3 fusion.32
  279.9 1.4 convolution_add_fusion.1
  281.6 1.3 convolution_add_fusion
  283.1 1.9 collective-permute-start.6
  285.0 6.3 %collective-permute-start.7 = (bf16[2,1,160,384]{3,2,1,0:T(8,128)(2,1)S(1)}, bf16[2,1,160,384]{3,2,1,0:T(8,128)(2,1)}, u32[]{:S(2)}, u32[]{:S(2)}) collective-permute-start(bf16[2,1,160,384]{3,2,1,0:T(8,128)(2,1)S(1)} %fusion.26), channel_id=1, source_target_pairs={{1,0},{2,1},{3,2},{4,3},{5,4},{6,5},{7,6},{8,7},{9,8},{10,9},{11,1... | collective-permute-start | bytes 737288 | tf_op jit(solution)/shard_map/ppermute | solution.py:21
  291.3 1.1 copy.26
  292.4 1.2 reshape.138
  293.6 1.0 collective-permute-done.6
  294.6 1.1 collective-permute-done.7
  295.7 1.2 pad_maximum_fusion
  297.1 2.6 broadcast_in_dim.5
  299.7 4.3 %reshape.135 = bf16[2,4,320,384]{3,2,1,0:T(8,128)(2,1)S(1)} reshape(bf16[2,4,160,2,384]{4,3,2,1,0:T(2,128)(2,1)} %broadcast_in_dim.5) | data formatting | bytes 3932160 | tf_op jit(solution)/shard_map/reshape | solution.py:86
  306.4 3.9 %fusion.13 = bf16[2,2,320,192]{2,3,1,0:T(8,128)(2,1)} fusion(bf16[2,2,320,3456]{3,2,1,0:T(8,128)(2,1)S(1)} %slice_dynamic-update-slice_fusion.3, bf16[3456,192,1,1]{0,1,2,3:T(8,128)(2,1)S(1)} %reshape.138), kind=kOutput, calls=%fused_computation.17 | convolution fusion | flops 1698938880 | bytes 10665984 | tf_op jit(solution)/shard_map/dot_general | solution.py:93
  (70 shorter events, 6.6 us)
Async XLA Ops:
  6.5 116.5 %all-gather.3.cloned.1.call-start = ((), (), s32[]{:S(2)}) async-start(), calls=%async_computation | async-start | bytes 10948608 | tf_op jit(solution)/shard_map/all_gather | solution.py:75
  8.4 234.2 %all-gather.5.cloned.1.call-start = ((), (), s32[]{:S(2)}) async-start(), calls=%async_computation.1 | async-start | bytes 10948608 | tf_op jit(solution)/shard_map/all_gather | solution.py:82
  12.6 7.5 %collective-permute-start = (bf16[2,1,160,384]{3,2,1,0:T(8,128)(2,1)S(1)}, bf16[2,1,160,384]{3,2,1,0:T(8,128)(2,1)S(1)}, u32[]{:S(2)}, u32[]{:S(2)}) collective-permute-start(bf16[2,1,160,384]{3,2,1,0:T(8,128)(2,1)S(1)} %fusion.25), channel_id=1, source_target_pairs={{0,32},{32,64},{64,96},{96,128},{128,160},{160,192},{192,224},{1,3... | collective-permute-start | bytes 737288 | tf_op jit(solution)/shard_map/ppermute | solution.py:10
  20.2 25.3 %collective-permute-start.1 = (bf16[4,1,160,384]{3,2,1,0:T(8,128)(2,1)S(1)}, bf16[4,1,160,384]{3,2,1,0:T(8,128)(2,1)S(1)}, u32[]{:S(2)}, u32[]{:S(2)}) collective-permute-start(bf16[4,1,160,384]{3,2,1,0:T(8,128)(2,1)S(1)} %pad_maximum_fusion.1), channel_id=1, source_target_pairs={{0,1},{1,2},{2,3},{3,4},{4,5},{5,6},{6,7},{7,8},{8,9},{9,10},{10,1... | collective-permute-start | bytes 1474568 | tf_op jit(solution)/shard_map/ppermute | solution.py:18
  24.0 22.5 %collective-permute-start.2 = (bf16[4,1,160,384]{3,2,1,0:T(8,128)(2,1)S(1)}, bf16[4,1,160,384]{3,2,1,0:T(8,128)(2,1)S(1)}, u32[]{:S(2)}, u32[]{:S(2)}) collective-permute-start(bf16[4,1,160,384]{3,2,1,0:T(8,128)(2,1)S(1)} %pad_maximum_fusion.1), channel_id=1, source_target_pairs={{1,0},{2,1},{3,2},{4,3},{5,4},{6,5},{7,6},{8,7},{9,8},{10,9},{11,1... | collective-permute-start | bytes 1474568 | tf_op jit(solution)/shard_map/ppermute | solution.py:21
  151.9 3.9 %copy-start.8 = (bf16[1,3,3,384,384]{4,3,2,1,0:T(8,128)(2,1)S(1)}, bf16[1,3,3,384,384]{4,3,2,1,0:T(8,128)(2,1)}, u32[]{:S(2)}) copy-start(bf16[1,3,3,384,384]{4,3,2,1,0:T(8,128)(2,1)} %copy.28) | copy-start | bytes 7962628
  151.9 3.9 %copy-start.10 = (bf16[2,1,160,3456]{3,2,1,0:T(8,128)(2,1)S(1)}, bf16[2,1,160,3456]{3,2,1,0:T(8,128)(2,1)}, u32[]{:S(2)}) copy-start(bf16[2,1,160,3456]{3,2,1,0:T(8,128)(2,1)} %get-tuple-element.16) | copy-start | bytes 6635524
  155.8 1.8 copy-start.7
  155.8 2.4 copy-start.9
  158.2 1.5 copy-start.14
  158.2 9.3 %copy-start.13 = (bf16[2,1,160,384]{3,2,1,0:T(8,128)(2,1)S(1)}, bf16[2,1,160,384]{3,2,1,0:T(8,128)(2,1)}, u32[]{:S(2)}) copy-start(bf16[2,1,160,384]{3,2,1,0:T(8,128)(2,1)} %param.10) | copy-start | bytes 737284
  160.0 7.6 %copy-start = (bf16[2,1,160,384]{3,2,1,0:T(8,128)(2,1)}, bf16[2,1,160,384]{3,2,1,0:T(8,128)(2,1)S(1)}, u32[]{:S(2)}) copy-start(bf16[2,1,160,384]{3,2,1,0:T(8,128)(2,1)S(1)} %multiply_convert_fusion) | copy-start | bytes 737284
  160.0 7.5 %collective-permute-start.3 = (bf16[2,1,160,384]{3,2,1,0:T(8,128)(2,1)S(1)}, bf16[2,1,160,384]{3,2,1,0:T(8,128)(2,1)S(1)}, u32[]{:S(2)}, u32[]{:S(2)}) collective-permute-start(bf16[2,1,160,384]{3,2,1,0:T(8,128)(2,1)S(1)} %multiply_convert_fusion), channel_id=1, source_target_pairs={{0,32},{32,64},{64,96},{96,128},{128,160},{160,192},{192,224},{1,3... | collective-permute-start | bytes 737288 | tf_op jit(solution)/shard_map/ppermute | solution.py:10
  167.6 0.9 copy-start.2
  168.5 103.0 %collective-permute-start.4 = (bf16[4,1,160,384]{3,2,1,0:T(8,128)(2,1)}, bf16[4,1,160,384]{3,2,1,0:T(8,128)(2,1)}, u32[]{:S(2)}, u32[]{:S(2)}) collective-permute-start(bf16[4,1,160,384]{3,2,1,0:T(8,128)(2,1)} %pad_maximum_fusion.2), channel_id=1, source_target_pairs={{0,1},{1,2},{2,3},{3,4},{4,5},{5,6},{6,7},{7,8},{8,9},{9,10},{10,1... | collective-permute-start | bytes 1474568 | tf_op jit(solution)/shard_map/ppermute | solution.py:18
  170.4 101.1 %collective-permute-start.5 = (bf16[4,1,160,384]{3,2,1,0:T(8,128)(2,1)}, bf16[4,1,160,384]{3,2,1,0:T(8,128)(2,1)}, u32[]{:S(2)}, u32[]{:S(2)}) collective-permute-start(bf16[4,1,160,384]{3,2,1,0:T(8,128)(2,1)} %pad_maximum_fusion.2), channel_id=1, source_target_pairs={{1,0},{2,1},{3,2},{4,3},{5,4},{6,5},{7,6},{8,7},{9,8},{10,9},{11,1... | collective-permute-start | bytes 1474568 | tf_op jit(solution)/shard_map/ppermute | solution.py:21
  271.4 3.3 %copy-start.1 = (bf16[2,1,160,384]{3,2,1,0:T(8,128)(2,1)S(1)}, bf16[2,1,160,384]{3,2,1,0:T(8,128)(2,1)}, u32[]{:S(2)}) copy-start(bf16[2,1,160,384]{3,2,1,0:T(8,128)(2,1)} %copy-done) | copy-start | bytes 737284
  271.4 3.3 %copy-start.3 = (bf16[2,1,160,384]{3,2,1,0:T(8,128)(2,1)S(1)}, bf16[2,1,160,384]{3,2,1,0:T(8,128)(2,1)}, u32[]{:S(2)}) copy-start(bf16[2,1,160,384]{3,2,1,0:T(8,128)(2,1)} %copy-done.2) | copy-start | bytes 737284
  276.4 1.8 copy-start.6
  278.1 1.7 copy-start.5
  279.9 1.7 copy-start.4
  281.6 1.4 copy-start.11
  281.6 9.6 %copy-start.12 = (bf16[3,3,384,192]{2,3,1,0:T(8,128)(2,1)S(1)}, bf16[3,3,384,192]{2,3,1,0:T(8,128)(2,1)}, u32[]{:S(2)}) copy-start(bf16[3,3,384,192]{2,3,1,0:T(8,128)(2,1)} %param.15) | copy-start | bytes 3981316
  283.1 11.6 %collective-permute-start.6 = (bf16[2,1,160,384]{3,2,1,0:T(8,128)(2,1)S(1)}, bf16[2,1,160,384]{3,2,1,0:T(8,128)(2,1)}, u32[]{:S(2)}, u32[]{:S(2)}) collective-permute-start(bf16[2,1,160,384]{3,2,1,0:T(8,128)(2,1)S(1)} %fusion.26), channel_id=1, source_target_pairs={{0,1},{1,2},{2,3},{3,4},{4,5},{5,6},{6,7},{7,8},{8,9},{9,10},{10,1... | collective-permute-start | bytes 737288 | tf_op jit(solution)/shard_map/ppermute | solution.py:18
  285.0 10.7 %collective-permute-start.7 = (bf16[2,1,160,384]{3,2,1,0:T(8,128)(2,1)S(1)}, bf16[2,1,160,384]{3,2,1,0:T(8,128)(2,1)}, u32[]{:S(2)}, u32[]{:S(2)}) collective-permute-start(bf16[2,1,160,384]{3,2,1,0:T(8,128)(2,1)S(1)} %fusion.26), channel_id=1, source_target_pairs={{1,0},{2,1},{3,2},{4,3},{5,4},{6,5},{7,6},{8,7},{9,8},{10,9},{11,1... | collective-permute-start | bytes 737288 | tf_op jit(solution)/shard_map/ppermute | solution.py:21
Sparse Core Ops, SparseCore 0:
  10.0 113.0 all-gather.2
  125.6 116.9 all-gather.4
where the time goes:
time: 319 us; the launch traced here: 317 us
  waiting for transfers between devices  168 us (53%)
  local copies, waits for them, and re-layouts  83.5 us (26%)
  starting transfers between devices  29.8 us (9%)
  matrix products  14.6 us (5%)
  between operations  13.9 us (4%)
  other arithmetic  7.16 us (2%)
    all_gather x1, waiting for transfers between devices, shards(): lax.all_gather(first_weight, 'rows', axis=4, tiled=True)  72.1 us
    all_gather x1, waiting for transfers between devices, shards(): lax.all_gather(second_weight, 'rows', axis=4, tiled=True)  66 us
    unnamed x61, local copies, waits for them, and re-layouts  53.7 us
    ppermute x3, starting transfers between devices, extended(): lax.ppermute(lax.slice_in_dim(block, 0, width, axis=dim), axis, backward)  18.2 us
    slice x2, local copies, waits for them, and re-layouts, conv_taps(): weight[time_tap].reshape(depth, outputs)  17.4 us
    ppermute x3, waiting for transfers between devices, extended(): lax.ppermute(lax.slice_in_dim(block, block.shape[dim] - width, None, axis...  16.8 us
    ppermute x2, waiting for transfers between devices, shifted(): return lax.ppermute(block, axis, route)  11.2 us
    dot_general x6, matrix products, conv_taps(): jnp.dot(block, weight[time_tap].reshape(depth, outputs), preferred_elemen...  10.8 us
  transfers between devices with their start and end apart: 10, of which 8 were waited for; matrix products, arithmetic and copies ran while one was open for 24% of the time, Pallas kernels for 0%

commit v1 on v0

v1 whole, which is shorter than its diff:
```python
import jax
import jax.numpy as jnp
from jax import lax
from jax.experimental import pallas as pl
from jax.experimental.pallas import tpu as pltpu
from jax.sharding import PartitionSpec as P

BF = jnp.bfloat16
F32 = jnp.float32
NT = (((1,), (1,)), ((), ()))
W = 160
C = 384
CO = 192
ND = 21
NQ = 5
NU = ND + NQ
NC = 41
TAPS = (((0,), (1, 2)), ((0, 1), (2,)))


def mod(a, n):
    return lax.rem(a + n, n)


def kernel(
    frames,
    cache0,
    cache1,
    gain0,
    gain1,
    win0,
    win1,
    up,
    out,
    zb0,
    zb1,
    w0,
    w1,
    xs0,
    xs1,
    bs,
    acc,
    cw,
    ph,
    il,
    ssem,
    rsem,
):
    tm = lax.axis_index("tm")
    r = lax.axis_index("rows")
    x, c = tm // 2, tm % 2
    y, z = r // 8, r % 8
    zdev = lambda d: (tm, y * 8 + mod(z + d, 8))
    ydev = lambda d: (tm, mod(y + d, 4) * 8 + z)
    xdev = lambda d: (mod(x + d, 4) * 2 + c, r)
    tdev = lambda d: (mod(tm + d, 8), r)
    rdev = lambda d: (tm, mod(r + d, 32))
    pair = (x * 2 + 1 - c, r)

    index = {}
    sends = []

    def copy(key, src, dst, dev):
        n = index.setdefault(key, len(index))
        return pltpu.make_async_remote_copy(
            src_ref=src,
            dst_ref=dst,
            send_sem=ssem.at[n],
            recv_sem=rsem.at[n],
            device_id=dev,
            device_id_type=pl.DeviceIdType.MESH,
        )

    def send(key, src, dev, dst=None, when=None):
        dst = src if dst is None else dst

        def go():
            copy(key, src, dst, dev).start()

        if when is None:
            go()
        else:
            pl.when(when)(go)
        sends.append((key, src, dst, dev, when))

    def recv(key, dst, when=None):
        def go():
            copy(key, dst, dst, pair).wait_recv()

        if when is None:
            go()
        else:
            pl.when(when)(go)

    zbs, ws, wins, xss = (zb0, zb1), (w0, w1), (win0, win1), (xs0, xs1)
    caches, gains = (cache0, cache1), (gain0, gain1)

    def prepare(v):
        zb, win = zbs[v], wins[v]
        zb[z] = jnp.zeros((NU, 16, 128), BF)

        def body(n, _):
            local = jnp.where(n < ND, n, n + NQ * x)
            u = jnp.where(c == 0, local, jnp.where(local == 40, 40, 41 + local))
            lane = pl.multiple_of((u % 3) * 128, 128)
            zb[z, n, 0:12, :] = win[u // 3, :, pl.ds(lane, 128)]
            return 0

        lax.fori_loop(0, NU, body, 0)

    def zblock(v, d):
        return zbs[v].at[mod(z + d, 8)]

    def zstart(v, s):
        send(("zf", v, s), zblock(v, 1 - s), zdev(1))
        if s < 4:
            send(("zb", v, s), zblock(v, s - 1), zdev(-1))

    def zwait(v, s):
        recv(("zf", v, s), zblock(v, -s))
        if s < 4:
            recv(("zb", v, s), zblock(v, s))

    row = lax.broadcasted_iota(jnp.int32, (96, 128), 0)
    col = lax.broadcasted_iota(jnp.int32, (96, 128), 1)
    squeeze = jnp.where(row + 4 * (row // 12) == col, 1.0, 0.0).astype(BF)
    ybase = lambda d: pl.multiple_of(mod(y + d, 4) * 96, 96)
    slot = lambda n: 41 * c + jnp.where(n < ND, n, n + NQ * x)

    def assemble(v, lo, hi):
        zb, w = zbs[v], ws[v]

        def one(n):
            w[slot(n), pl.ds(ybase(0), 96), :] = jnp.dot(
                squeeze, zb[:, n].reshape(128, 128), preferred_element_type=F32
            ).astype(BF)

        def body(n, _):
            one(lo + 2 * n)
            one(lo + 2 * n + 1)
            return 0

        lax.fori_loop(0, (hi - lo) // 2, body, 0)
        if (hi - lo) % 2:
            one(jnp.int32(hi - 1))

    dbase = 41 * c
    qbase = lambda d: 41 * c + ND + NQ * mod(x + d, 4)
    segment = {"q": (qbase(0), NQ, 3), "d": (dbase, ND, 11)}

    def yview(v, g, d, part):
        base, count, cut = segment[g]
        lo, n = ((0, count), (0, cut), (cut, count - cut))[part]
        return ws[v].at[pl.ds(base + lo, n), pl.ds(ybase(d), 96), :]

    def ystart1(v, g):
        send(("yf1", v, g), yview(v, g, 0, 0), ydev(1))
        send(("yb1", v, g), yview(v, g, 0, 0), ydev(-1))

    def ystart2(v, g):
        recv(("yf1", v, g), yview(v, g, -1, 0))
        send(("yf2", v, g), yview(v, g, -1, 1), ydev(1))
        recv(("yb1", v, g), yview(v, g, 1, 0))
        send(("yb2", v, g), yview(v, g, 1, 2), ydev(-1))

    def ywait2(v, g):
        recv(("yf2", v, g), yview(v, g, -2, 1))
        recv(("yb2", v, g), yview(v, g, 2, 2))

    def xview(v, d, part):
        lo, n = ((0, NQ), (0, 3), (3, 2))[part]
        return ws[v].at[pl.ds(qbase(d) + lo, n)]

    def cview(v, core, lo, n):
        return ws[v].at[pl.ds(41 * core + lo, n)]

    def xstart1(v):
        send(("xf1", v), xview(v, 0, 0), xdev(1))
        send(("xb1", v), xview(v, 0, 0), xdev(-1))

    def xstart2(v):
        recv(("xf1", v), xview(v, -1, 0))
        send(("xf2", v), xview(v, -1, 1), xdev(1))
        recv(("xb1", v), xview(v, 1, 0))
        send(("xb2", v), xview(v, 1, 2), xdev(-1))

    def xwait2(v):
        recv(("xf2", v), xview(v, -2, 1))
        recv(("xb2", v), xview(v, 2, 2))

    def handd(v):
        send(("cd", v), cview(v, c, 0, ND), pair)

    def handq(v):
        send(("cq", v), cview(v, c, ND, NC - ND), pair)

    def handwait(v):
        recv(("cd", v), cview(v, 1 - c, 0, ND))
        recv(("cq", v), cview(v, 1 - c, ND, NC - ND))

    def normed(v, values):
        scale = lax.rsqrt(jnp.mean(values * values, axis=-1, keepdims=True) + 1e-06)
        return jax.nn.silu(values * scale * gains[v][...]).astype(BF)

    inner_lo, inner_hi, later, first = r > 0, r < 31, tm < 7, tm == 0

    def halo_start(v):
        xs = xss[v]
        own = xs.at[1, 1, pl.ds(2, 2)]
        send(("up", v), own, rdev(1), xs.at[1, 0, pl.ds(2, 2)], inner_hi)
        send(("dn", v), own, rdev(-1), xs.at[1, 2, pl.ds(2, 2)], inner_lo)
        send(("t1", v), own, tdev(1), xs.at[1, 1, pl.ds(0, 2)], later)

    def cache_start(v):
        xs = xss[v]

        @pl.when(first)
        def _():
            xs[1, 1, 0:2] = caches[v][...]

        old = xs.at[1, 1, pl.ds(0, 2)]
        send(("cu", v), old, rdev(1), xs.at[1, 0, pl.ds(0, 2)], first & inner_hi)
        send(("cn", v), old, rdev(-1), xs.at[1, 2, pl.ds(0, 2)], first & inner_lo)

        @pl.when(r == 0)
        def _():
            xs[1, 0] = jnp.zeros((4, W, C), BF)

        @pl.when(r == 31)
        def _():
            xs[1, 2] = jnp.zeros((4, W, C), BF)

    def halo_pass(v):
        xs = xss[v]
        low, high = xs.at[1, 0, pl.ds(2, 2)], xs.at[1, 2, pl.ds(2, 2)]
        recv(("up", v), low, inner_lo)
        send(("t0", v), low, tdev(1), xs.at[1, 0, pl.ds(0, 2)], later & inner_lo)
        recv(("dn", v), high, inner_hi)
        send(("t2", v), high, tdev(1), xs.at[1, 2, pl.ds(0, 2)], later & inner_hi)

    def halo_wait(v):
        xs = xss[v]
        old = [xs.at[1, j, pl.ds(0, 2)] for j in range(3)]
        recv(("t1", v), old[1], tm > 0)
        recv(("t0", v), old[0], (tm > 0) & inner_lo)
        recv(("t2", v), old[2], (tm > 0) & inner_hi)
        recv(("cu", v), old[0], first & inner_lo)
        recv(("cn", v), old[2], first & inner_hi)

    def shift(buf, j, f):
        v = buf[1, j, f].astype(F32)
        at = lax.broadcasted_iota(jnp.int32, v.shape, 0)
        buf[0, j, f] = jnp.where(at == 0, 0.0, pltpu.roll(v, 1, 0)).astype(BF)
        buf[2, j, f] = jnp.where(at == W - 1, 0.0, pltpu.roll(v, W - 1, 0)).astype(BF)

    def shifts(buf, js, f0, n):
        for j in js:

            def body(f, _):
                shift(buf, j, f0 + f)
                return 0

            lax.fori_loop(0, n, body, 0)

    def conv(v, lo, hi):
        xs, w = xss[v], ws[v]

        def body(ij, _):
            i, j = ij // 3, ij % 3
            lhs = jnp.concatenate(
                [xs[k, j, pl.ds(i, 2)].reshape(2 * W, C) for k in range(3)], axis=1
            )
            rhs = jnp.concatenate([w[9 * ij + u] for u in range(9)], axis=1)
            acc[...] += lax.dot_general(lhs, rhs, NT, preferred_element_type=F32)
            return 0

        lax.fori_loop(lo, hi, body, 0)

    def combine():
        for a in range(2):
            for p in range(2):
                for b in range(2):
                    for q in range(2):
                        total = sum(
                            up[j, k].astype(F32) for j in TAPS[a][p] for k in TAPS[b][q]
                        )
                        cw[a, p, b, q] = total.astype(BF)

    def phase(a, b, p):
        lhs = jnp.concatenate(
            [bs[b + q, a + p].reshape(2 * W, C) for q in range(2)], axis=1
        )
        rhs = jnp.concatenate([cw[a, p, b, q] for q in range(2)], axis=1)
        return lax.dot_general(lhs, rhs, NT, preferred_element_type=F32)

    prepare(0)
    barrier = pltpu.get_barrier_semaphore()
    for near in (zdev, ydev, xdev, tdev, rdev):
        for d in (1, -1):
            pl.semaphore_signal(
                barrier, inc=1, device_id=near(d), device_id_type=pl.DeviceIdType.MESH
            )
    pl.semaphore_wait(barrier, 10)

    zstart(0, 1)
    xs0[1, 1, 2:4] = normed(0, frames[...].astype(F32).reshape(2 * W, C)).reshape(2, W, C)
    halo_start(0)
    cache_start(0)
    zwait(0, 1)
    zstart(0, 2)
    cache_start(1)
    prepare(1)
    zwait(0, 2)
    zstart(0, 3)
    shifts(xs0, (1,), 2, 2)
    halo_pass(0)
    zwait(0, 3)
    zstart(0, 4)
    combine()
    zwait(0, 4)
    zstart(1, 1)
    assemble(0, ND, NU)
    ystart1(0, "q")
    assemble(0, 0, ND)
    ystart1(0, "d")
    zwait(1, 1)
    zstart(1, 2)
    ystart2(0, "q")
    zwait(1, 2)
    zstart(1, 3)
    ywait2(0, "q")
    xstart1(0)
    zwait(1, 3)
    zstart(1, 4)
    halo_wait(0)
    shifts(xs0, (0, 2), 2, 2)
    shifts(xs0, (0, 1, 2), 0, 2)
    zwait(1, 4)
    ystart2(0, "d")
    assemble(1, ND, NU)
    ystart1(1, "q")
    assemble(1, 0, ND)
    ystart1(1, "d")
    xstart2(0)
    ywait2(0, "d")
    handd(0)
    ystart2(1, "q")
    ywait2(1, "q")
    xwait2(0)
    handq(0)
    xstart1(1)
    acc[...] = jnp.zeros_like(acc)
    handwait(0)
    conv(0, 0, 9)
    xs1[1, 1, 2:4] = normed(1, acc[...].astype(BF).astype(F32)).reshape(2, W, C)
    halo_start(1)
    ystart2(1, "d")
    xstart2(1)
    shifts(xs1, (1,), 2, 2)
    halo_pass(1)
    ywait2(1, "d")
    handd(1)
    xwait2(1)
    handq(1)
    halo_wait(1)
    shifts(xs1, (0, 2), 2, 2)
    shifts(xs1, (0, 1, 2), 0, 2)
    acc[...] = frames[...].astype(F32).reshape(2 * W, C)
    handwait(1)
    conv(1, 0, 9)

    bs[1, 1] = acc[...].astype(BF).reshape(2, W, C)
    send("bu", bs.at[1, 1], rdev(1), bs.at[1, 0], inner_hi)
    send("bd", bs.at[1, 1], rdev(-1), bs.at[1, 2], inner_lo)

    @pl.when(r == 0)
    def _():
        bs[1, 0] = jnp.zeros((2, W, C), BF)

    @pl.when(r == 31)
    def _():
        bs[1, 2] = jnp.zeros((2, W, C), BF)

    shifts(bs, (1,), 0, 2)
    for a in range(2):
        for b in range(2):
            ph[a, b] = phase(a, b, 1 - a)
    recv("bu", bs.at[1, 0], inner_lo)
    recv("bd", bs.at[1, 2], inner_hi)
    shifts(bs, (0, 2), 0, 2)
    for a in range(2):
        for b in range(2):
            total = ph[a, b] + phase(a, b, a)
            for f in range(2):
                part = total[f * W : (f + 1) * W]
                il[f, pl.ds(b, W, stride=2), :] = part[:, :128]
                il[2 + f, pl.ds(b, W, stride=2), 0:64] = part[:, 128:]
        for f in range(2):
            out[f, a, :, 0:128] = il[f].astype(BF)
            out[f, a, :, 128:192] = il[2 + f, :, 0:64].astype(BF)

    for key, src, dst, dev, when in sends:
        done = lambda k=key, s=src, d=dst, e=dev: copy(k, s, d, e).wait_send()
        if when is None:
            done()
        else:
            pl.when(when)(done)


def shards(frames, cache0, cache1, gain0, gain1, first, second, upsample):
    vmem = pl.BlockSpec(memory_space=pltpu.VMEM)
    block = lambda v: v.reshape(2, W, C)
    flip = lambda v: jnp.swapaxes(v, 3, 4).reshape(27, 12, C)
    return pl.pallas_call(
        kernel,
        out_shape=jax.ShapeDtypeStruct((2, 2, 2 * W, CO), BF),
        in_specs=[vmem] * 8,
        out_specs=vmem,
        scratch_shapes=[
            pltpu.VMEM((8, NU, 16, 128), BF),
            pltpu.VMEM((8, NU, 16, 128), BF),
            pltpu.VMEM((2 * NC, C, 128), BF),
            pltpu.VMEM((2 * NC, C, 128), BF),
            pltpu.VMEM((3, 3, 4, W, C), BF),
            pltpu.VMEM((3, 3, 4, W, C), BF),
            pltpu.VMEM((3, 3, 2, W, C), BF),
            pltpu.VMEM((2 * W, C), F32),
            pltpu.VMEM((2, 2, 2, 2, CO, C), BF),
            pltpu.VMEM((2, 2, 2 * W, CO), F32),
            pltpu.VMEM((4, 2 * W, 128), F32),
            pltpu.SemaphoreType.DMA((64,)),
            pltpu.SemaphoreType.DMA((64,)),
        ],
        compiler_params=pltpu.CompilerParams(
            collective_id=0, has_side_effects=True, vmem_limit_bytes=60 << 20
        ),
    )(
        block(frames),
        block(cache0),
        block(cache1),
        gain0.reshape(1, C),
        gain1.reshape(1, C),
        flip(first),
        flip(second),
        jnp.swapaxes(upsample, 2, 3),
    )


def solution(mesh):
    in_specs = (
        P("tm", "rows", None, None),
        P(None, "rows", None, None),
        P(None, "rows", None, None),
        P(),
        P(),
        P(None, None, None, None, "rows"),
        P(None, None, None, None, "rows"),
        P(),
    )
    out_specs = P("tm", "rows", None, None)
    return jax.shard_map(shards, mesh=mesh, in_specs=in_specs, out_specs=out_specs, check_vma=False)
```

time: 319 us -> 115 us (0.36)
  waiting for transfers between devices: 168 us -> 0 us
  Pallas kernels: 0 us -> 110 us
  local copies, waits for them, and re-layouts: 83.5 us -> 4.64 us
  starting transfers between devices: 29.8 us -> 0 us
  matrix products: 14.6 us -> 0 us
  between operations: 13.9 us -> 0.01 us
  other arithmetic: 7.16 us -> 0 us
    all_gather x2 -> x0, waiting for transfers between devices: 138 us -> none  [the longest x1 72.1 us: shards(): lax.all_gather(first_weight, 'rows', axis=4, tiled=True)]
    pallas_call x0 -> x1, Pallas kernels: none -> 110 us  [shards(): pl.pallas_call(kernel, out_shape=jax.ShapeDtypeStruct((2, 2, 2 * W, CO),...]
    unnamed x61 -> x0, local copies, waits for them, and re-layouts: 53.7 us -> none
    ppermute x8 -> x0, waiting for transfers between devices: 30 us -> none  [the longest x3 16.8 us: extended(): lax.ppermute(lax.slice_in_dim(block, block.shape[dim] - width, None, axis...]
    ppermute x8 -> x0, starting transfers between devices: 29.7 us -> none  [the longest x3 18.2 us: extended(): lax.ppermute(lax.slice_in_dim(block, 0, width, axis=dim), axis, backward)]
    slice x5 -> x0, local copies, waits for them, and re-layouts: 20.9 us -> none  [the longest x2 17.4 us: conv_taps(): weight[time_tap].reshape(depth, outputs)]
    dot_general x7 -> x0, matrix products: 14.6 us -> none  [the longest x6 10.8 us: conv_taps(): jnp.dot(block, weight[time_tap].reshape(depth, outputs), preferred_elemen...]
    concatenate x5 -> x0, other arithmetic: 4.36 us -> none  [the longest x3 3.45 us: extended(): block = jnp.concatenate([low, block, high], axis=dim)]
  transfers between devices with their start and end apart: 10 -> 0, of which waited for: 8 -> 0; matrix products, arithmetic and copies ran while one was open for 24% -> 0% of each run, Pallas kernels for 0% -> 0%
where the time goes in v1:
time: 115 us
  Pallas kernels  110 us (96%)
  local copies, waits for them, and re-layouts  4.64 us (4%)
    pallas_call x1, Pallas kernels, shards(): pl.pallas_call(kernel, out_shape=jax.ShapeDtypeStruct((2, 2, 2 * W, CO),...  110 us

profile of v1, /device:TPU:10, one launch (start us, length us, event | category | flops | bytes accessed | tf_op | source)
XLA Modules:
  0.0 114.8 jit_solution(7339062183391038584)
XLA Ops:
  0.0 1.2 %reshape.24.gain0 = f32[1,384]{1,0:T(1,128)} reshape(f32[384]{0:T(512)} %param.11) | data formatting | bytes 3072 | tf_op jit(solution)/shard_map/reshape | solution.py:441
  1.2 1.2 %reshape.25.gain1 = f32[1,384]{1,0:T(1,128)} reshape(f32[384]{0:T(512)} %param.12) | data formatting | bytes 3072 | tf_op jit(solution)/shard_map/reshape | solution.py:442
  2.5 110.2 %shard_map.82 = bf16[2,2,320,192]{3,2,1,0:T(8,128)(2,1)} custom-call(bf16[2,160,384]{2,1,0:T(8,128)(2,1)} %bitcast.13, bf16[2,160,384]{2,1,0:T(8,128)(2,1)} %bitcast.14, bf16[2,160,384]{2,1,0:T(8,128)(2,1)} %bitcast.15, f32[1,384]{1,0:T(1,128)} %reshape.24.gain0, f32[1,384]{1,0:T(1,128)} %reshape.25.gain1, bf16[27,12,384]{2,1,0:T(8,128)(2,1)} %bitcast.11, ...), custom_call_target="tpu_custom_call" | custom-call | tf_op jit(solution)/shard_map/pallas_call | solution.py:414
  112.7 2.2 %copy.9 = bf16[2,2,320,192]{2,3,1,0:T(8,128)(2,1)} copy(bf16[2,2,320,192]{3,2,1,0:T(8,128)(2,1)} %shard_map.82) | data formatting | bytes 983040 | tf_op jit(solution)/shard_map/pallas_call | solution.py:414

commit v2 on v1

--- a/solution.py
+++ b/solution.py
@@ -11,10 +11,11 @@
 W = 160
 C = 384
 CO = 192
-ND = 21
-NQ = 5
-NU = ND + NQ
+ND = (21, 25)
+NQ = (5, 4)
 NC = 41
+NB = 9
+CUTS = ((12, 0), (9, 7))
 TAPS = (((0,), (1, 2)), ((0, 1), (2,)))
 
 
@@ -95,121 +96,161 @@
     zbs, ws, wins, xss = (zb0, zb1), (w0, w1), (win0, win1), (xs0, xs1)
     caches, gains = (cache0, cache1), (gain0, gain1)
 
+    chunks = []
+    for d, q, (nc, ne) in zip(ND, NQ, CUTS):
+        chunks.append(
+            {
+                "b": (0, NB),
+                "c": (NB, nc),
+                "e": (NB + nc, ne),
+                "r": (NB, nc + ne),
+                "q": (d, q),
+            }
+        )
+
+    def unit(v, n):
+        local = jnp.where(n < ND[v], n, n + NQ[v] * x)
+        second = jnp.where(
+            local < 18,
+            45 + local,
+            jnp.where(
+                local < 21,
+                23 + local,
+                jnp.where(local == 21, 44, jnp.where(local == 40, 40, 41 + local)),
+            ),
+        )
+        return jnp.where(c == 0, local, second)
+
     def prepare(v):
         zb, win = zbs[v], wins[v]
-        zb[z] = jnp.zeros((NU, 16, 128), BF)
+        zb[z] = jnp.zeros((ND[v] + NQ[v], 16, 128), BF)
 
         def body(n, _):
-            local = jnp.where(n < ND, n, n + NQ * x)
-            u = jnp.where(c == 0, local, jnp.where(local == 40, 40, 41 + local))
+            u = unit(v, n)
             lane = pl.multiple_of((u % 3) * 128, 128)
             zb[z, n, 0:12, :] = win[u // 3, :, pl.ds(lane, 128)]
             return 0
 
-        lax.fori_loop(0, NU, body, 0)
-
-    def zblock(v, d):
-        return zbs[v].at[mod(z + d, 8)]
-
-    def zstart(v, s):
-        send(("zf", v, s), zblock(v, 1 - s), zdev(1))
-        if s < 4:
-            send(("zb", v, s), zblock(v, s - 1), zdev(-1))
-
-    def zwait(v, s):
-        recv(("zf", v, s), zblock(v, -s))
-        if s < 4:
-            recv(("zb", v, s), zblock(v, s))
+        lax.fori_loop(0, ND[v] + NQ[v], body, 0)
+
+    def split(v, g, part):
+        lo, n = chunks[v][g]
+        cut = (n + 1) // 2
+        return ((lo, n), (lo, cut), (lo + cut, n - cut))[part]
+
+    def zview(v, g, d, part=0):
+        return zbs[v].at[mod(z + d, 8), pl.ds(*split(v, g, part))]
+
+    def zstart(v, g):
+        for d in (2, -2, 1, -1):
+            send(("z", v, g, d), zview(v, g, 0), zdev(d))
+
+    def zpass(v, g):
+        for d in (2, -2):
+            part = 1 if d > 0 else 2
+            recv(("z", v, g, d), zview(v, g, -d))
+            send(("z", v, g, 2 * d), zview(v, g, -d, part), zdev(d))
+            send(("z", v, g, 3 * d // 2), zview(v, g, -d), zdev(d // 2))
+
+    def zwait(v, g):
+        for d in (1, -1, 3, -3):
+            recv(("z", v, g, d), zview(v, g, -d))
+        for d in (4, -4):
+            recv(("z", v, g, d), zview(v, g, -d, 1 if d > 0 else 2))
 
     row = lax.broadcasted_iota(jnp.int32, (96, 128), 0)
     col = lax.broadcasted_iota(jnp.int32, (96, 128), 1)
     squeeze = jnp.where(row + 4 * (row // 12) == col, 1.0, 0.0).astype(BF)
     ybase = lambda d: pl.multiple_of(mod(y + d, 4) * 96, 96)
-    slot = lambda n: 41 * c + jnp.where(n < ND, n, n + NQ * x)
-
-    def assemble(v, lo, hi):
-        zb, w = zbs[v], ws[v]
-
-        def one(n):
-            w[slot(n), pl.ds(ybase(0), 96), :] = jnp.dot(
-                squeeze, zb[:, n].reshape(128, 128), preferred_element_type=F32
-            ).astype(BF)
-
-        def body(n, _):
-            one(lo + 2 * n)
-            one(lo + 2 * n + 1)
-            return 0
-
-        lax.fori_loop(0, (hi - lo) // 2, body, 0)
-        if (hi - lo) % 2:
-            one(jnp.int32(hi - 1))
-
-    dbase = 41 * c
-    qbase = lambda d: 41 * c + ND + NQ * mod(x + d, 4)
-    segment = {"q": (qbase(0), NQ, 3), "d": (dbase, ND, 11)}
+    qbase = lambda v, core, d: 41 * core + ND[v] + NQ[v] * mod(x + d, 4)
+
+    def base(v, g, core, d=0):
+        return qbase(v, core, d) if g == "q" else 41 * core + chunks[v][g][0]
+
+    def assemble(v, g):
+        lo, count = chunks[v][g]
+        blocks = [zbs[v][:, lo + n].reshape(128, 128) for n in range(count)]
+        rows = jnp.dot(
+            squeeze, jnp.concatenate(blocks, axis=1), preferred_element_type=F32
+        ).astype(BF)
+        first = base(v, g, c)
+        for n in range(count):
+            ws[v][first + n, pl.ds(ybase(0), 96), :] = rows[:, 128 * n : 128 * n + 128]
 
     def yview(v, g, d, part):
-        base, count, cut = segment[g]
-        lo, n = ((0, count), (0, cut), (cut, count - cut))[part]
-        return ws[v].at[pl.ds(base + lo, n), pl.ds(ybase(d), 96), :]
-
-    def ystart1(v, g):
+        lo, n = split(v, g, part)
+        lo = lo - chunks[v][g][0]
+        return ws[v].at[pl.ds(base(v, g, c) + lo, n), pl.ds(ybase(d), 96), :]
+
+    def ystart(v, g):
         send(("yf1", v, g), yview(v, g, 0, 0), ydev(1))
         send(("yb1", v, g), yview(v, g, 0, 0), ydev(-1))
 
-    def ystart2(v, g):
+    def ypass(v, g):
         recv(("yf1", v, g), yview(v, g, -1, 0))
         send(("yf2", v, g), yview(v, g, -1, 1), ydev(1))
         recv(("yb1", v, g), yview(v, g, 1, 0))
         send(("yb2", v, g), yview(v, g, 1, 2), ydev(-1))
 
-    def ywait2(v, g):
+    def ywait(v, g):
         recv(("yf2", v, g), yview(v, g, -2, 1))
         recv(("yb2", v, g), yview(v, g, 2, 2))
 
     def xview(v, d, part):
-        lo, n = ((0, NQ), (0, 3), (3, 2))[part]
-        return ws[v].at[pl.ds(qbase(d) + lo, n)]
-
-    def cview(v, core, lo, n):
-        return ws[v].at[pl.ds(41 * core + lo, n)]
-
-    def xstart1(v):
-        send(("xf1", v), xview(v, 0, 0), xdev(1))
-        send(("xb1", v), xview(v, 0, 0), xdev(-1))
-
-    def xstart2(v):
-        recv(("xf1", v), xview(v, -1, 0))
-        send(("xf2", v), xview(v, -1, 1), xdev(1))
-        recv(("xb1", v), xview(v, 1, 0))
-        send(("xb2", v), xview(v, 1, 2), xdev(-1))
-
-    def xwait2(v):
-        recv(("xf2", v), xview(v, -2, 1))
-        recv(("xb2", v), xview(v, 2, 2))
-
-    def handd(v):
-        send(("cd", v), cview(v, c, 0, ND), pair)
-
-    def handq(v):
-        send(("cq", v), cview(v, c, ND, NC - ND), pair)
-
-    def handwait(v):
-        recv(("cd", v), cview(v, 1 - c, 0, ND))
-        recv(("cq", v), cview(v, 1 - c, ND, NC - ND))
+        lo, n = ((0, 1), (1, NQ[v] - 1))[part - 1]
+        return ws[v].at[pl.ds(qbase(v, c, d) + lo, n)]
+
+    def xstart(v):
+        for first in (1, 2):
+            send(("xf", v, first), xview(v, 0, first), xdev(1))
+            send(("xb", v, 3 - first), xview(v, 0, 3 - first), xdev(-1))
+
+    def xpass(v, d):
+        key, part = ("xf", 1) if d > 0 else ("xb", 2)
+        recv((key, v, part), xview(v, -d, part))
+        send((key, v, 3), xview(v, -d, part), xdev(d))
+
+    def xsides(v):
+        recv(("xf", v, 2), xview(v, -1, 2))
+        recv(("xb", v, 1), xview(v, 1, 1))
+
+    def xwait(v):
+        recv(("xf", v, 3), xview(v, -2, 1))
+        recv(("xb", v, 3), xview(v, 2, 2))
+
+    def cview(v, g, core, d=0):
+        return ws[v].at[pl.ds(base(v, g, core, d), chunks[v][g][1])]
+
+    def hand(v, g, d=0):
+        send(("c", v, g, d), cview(v, g, c, d), pair)
+
+    def taken(v, g, d=0):
+        recv(("c", v, g, d), cview(v, g, 1 - c, d))
+
+    def alltaken(v):
+        for d in (0, 1, -1, 2):
+            taken(v, "q", d)
 
     def normed(v, values):
         scale = lax.rsqrt(jnp.mean(values * values, axis=-1, keepdims=True) + 1e-06)
         return jax.nn.silu(values * scale * gains[v][...]).astype(BF)
 
     inner_lo, inner_hi, later, first = r > 0, r < 31, tm < 7, tm == 0
+
+    def halo_row(v):
+        xs = xss[v]
+        own = xs.at[1, 1, pl.ds(2, 2)]
+        send(("t1", v), own, tdev(1), xs.at[1, 1, pl.ds(0, 2)], later)
 
     def halo_start(v):
         xs = xss[v]
         own = xs.at[1, 1, pl.ds(2, 2)]
         send(("up", v), own, rdev(1), xs.at[1, 0, pl.ds(2, 2)], inner_hi)
         send(("dn", v), own, rdev(-1), xs.at[1, 2, pl.ds(2, 2)], inner_lo)
-        send(("t1", v), own, tdev(1), xs.at[1, 1, pl.ds(0, 2)], later)
+        away = later & (c == 1)
+        below, above = (mod(tm + 1, 8), mod(r + 1, 32)), (mod(tm + 1, 8), mod(r - 1, 32))
+        send(("t0", v), own, below, xs.at[1, 0, pl.ds(0, 2)], away & inner_hi)
+        send(("t2", v), own, above, xs.at[1, 2, pl.ds(0, 2)], away & inner_lo)
 
     def cache_start(v):
         xs = xss[v]
@@ -234,9 +275,9 @@
         xs = xss[v]
         low, high = xs.at[1, 0, pl.ds(2, 2)], xs.at[1, 2, pl.ds(2, 2)]
         recv(("up", v), low, inner_lo)
-        send(("t0", v), low, tdev(1), xs.at[1, 0, pl.ds(0, 2)], later & inner_lo)
+        send(("t0", v), low, tdev(1), xs.at[1, 0, pl.ds(0, 2)], (c == 0) & inner_lo)
         recv(("dn", v), high, inner_hi)
-        send(("t2", v), high, tdev(1), xs.at[1, 2, pl.ds(0, 2)], later & inner_hi)
+        send(("t2", v), high, tdev(1), xs.at[1, 2, pl.ds(0, 2)], (c == 0) & inner_hi)
 
     def halo_wait(v):
         xs = xss[v]
@@ -262,19 +303,24 @@
 
             lax.fori_loop(0, n, body, 0)
 
-    def conv(v, lo, hi):
+    def conv(v, *pieces):
         xs, w = xss[v], ws[v]
 
-        def body(ij, _):
+        def body(n, _):
+            ij = jnp.int32(pieces[0])
+            for m in range(1, len(pieces)):
+                ij = jnp.where(n == m, pieces[m], ij)
             i, j = ij // 3, ij % 3
+            low = 9 * ij - jnp.where((ij == 5) | (ij == 6), 4, 0)
+            high = low + jnp.where(ij == 4, 18, 0)
             lhs = jnp.concatenate(
                 [xs[k, j, pl.ds(i, 2)].reshape(2 * W, C) for k in range(3)], axis=1
             )
-            rhs = jnp.concatenate([w[9 * ij + u] for u in range(9)], axis=1)
+            rhs = jnp.concatenate([w[(low if u < 5 else high) + u] for u in range(9)], axis=1)
             acc[...] += lax.dot_general(lhs, rhs, NT, preferred_element_type=F32)
             return 0
 
-        lax.fori_loop(lo, hi, body, 0)
+        lax.fori_loop(0, len(pieces), body, 0)
 
     def combine():
         for a in range(2):
@@ -293,81 +339,120 @@
         rhs = jnp.concatenate([cw[a, p, b, q] for q in range(2)], axis=1)
         return lax.dot_general(lhs, rhs, NT, preferred_element_type=F32)
 
+    barrier = pltpu.get_barrier_semaphore()
+    near = [f(d) for f in (zdev, ydev, xdev, tdev, rdev) for d in (1, -1)]
+    near += [zdev(2), zdev(-2)]
+    near += [(mod(tm + d, 8), mod(r + e, 32)) for d in (1, -1) for e in (1, -1)]
+    for dev in near:
+        pl.semaphore_signal(barrier, inc=1, device_id=dev, device_id_type=pl.DeviceIdType.MESH)
     prepare(0)
-    barrier = pltpu.get_barrier_semaphore()
-    for near in (zdev, ydev, xdev, tdev, rdev):
-        for d in (1, -1):
-            pl.semaphore_signal(
-                barrier, inc=1, device_id=near(d), device_id_type=pl.DeviceIdType.MESH
-            )
-    pl.semaphore_wait(barrier, 10)
-
-    zstart(0, 1)
+    pl.semaphore_wait(barrier, len(near))
+
+    zstart(0, "q")
     xs0[1, 1, 2:4] = normed(0, frames[...].astype(F32).reshape(2 * W, C)).reshape(2, W, C)
+    halo_row(0)
+    zpass(0, "q")
+    zstart(0, "b")
+    zstart(0, "c")
+    zwait(0, "q")
+    assemble(0, "q")
+    ystart(0, "q")
+    zpass(0, "b")
+    prepare(1)
+    zpass(0, "c")
+    zwait(0, "b")
+    assemble(0, "b")
+    ypass(0, "q")
+    ystart(0, "b")
+    zwait(0, "c")
+    assemble(0, "c")
+    ystart(0, "c")
+    ywait(0, "q")
+    xstart(0)
+    hand(0, "q", 0)
+    zstart(1, "q")
+    zstart(1, "b")
     halo_start(0)
     cache_start(0)
-    zwait(0, 1)
-    zstart(0, 2)
-    cache_start(1)
-    prepare(1)
-    zwait(0, 2)
-    zstart(0, 3)
+    zstart(1, "r")
+    ypass(0, "b")
+    xpass(0, 1)
+    zpass(1, "q")
+    zpass(1, "b")
     shifts(xs0, (1,), 2, 2)
+    ypass(0, "c")
+    zwait(1, "q")
+    assemble(1, "q")
+    ystart(1, "q")
+    xpass(0, -1)
+    ywait(0, "b")
+    hand(0, "b")
     halo_pass(0)
-    zwait(0, 3)
-    zstart(0, 4)
-    combine()
-    zwait(0, 4)
-    zstart(1, 1)
-    assemble(0, ND, NU)
-    ystart1(0, "q")
-    assemble(0, 0, ND)
-    ystart1(0, "d")
-    zwait(1, 1)
-    zstart(1, 2)
-    ystart2(0, "q")
-    zwait(1, 2)
-    zstart(1, 3)
-    ywait2(0, "q")
-    xstart1(0)
-    zwait(1, 3)
-    zstart(1, 4)
+    zwait(1, "b")
+    assemble(1, "b")
+    ystart(1, "b")
+    ywait(0, "c")
+    hand(0, "c")
+    xsides(0)
+    hand(0, "q", 1)
+    hand(0, "q", -1)
+    zpass(1, "r")
+    ypass(1, "q")
+    acc[...] = jnp.zeros_like(acc)
     halo_wait(0)
     shifts(xs0, (0, 2), 2, 2)
     shifts(xs0, (0, 1, 2), 0, 2)
-    zwait(1, 4)
-    ystart2(0, "d")
-    assemble(1, ND, NU)
-    ystart1(1, "q")
-    assemble(1, 0, ND)
-    ystart1(1, "d")
-    xstart2(0)
-    ywait2(0, "d")
-    handd(0)
-    ystart2(1, "q")
-    ywait2(1, "q")
-    xwait2(0)
-    handq(0)
-    xstart1(1)
-    acc[...] = jnp.zeros_like(acc)
-    handwait(0)
-    conv(0, 0, 9)
+    taken(0, "b")
+    conv(0, 0, 5)
+    xwait(0)
+    hand(0, "q", 2)
+    ywait(1, "q")
+    xstart(1)
+    hand(1, "q", 0)
+    taken(0, "c")
+    conv(0, 1, 6)
+    zwait(1, "r")
+    assemble(1, "c")
+    ystart(1, "c")
+    assemble(1, "e")
+    ystart(1, "e")
+    ypass(1, "b")
+    alltaken(0)
+    conv(0, 2, 3, 4, 7, 8)
     xs1[1, 1, 2:4] = normed(1, acc[...].astype(BF).astype(F32)).reshape(2, W, C)
+    halo_row(1)
     halo_start(1)
-    ystart2(1, "d")
-    xstart2(1)
+    cache_start(1)
+    xpass(1, 1)
+    acc[...] = frames[...].astype(F32).reshape(2 * W, C)
     shifts(xs1, (1,), 2, 2)
+    xpass(1, -1)
+    ypass(1, "c")
+    combine()
+    ywait(1, "b")
+    hand(1, "b")
+    xsides(1)
+    hand(1, "q", 1)
+    hand(1, "q", -1)
     halo_pass(1)
-    ywait2(1, "d")
-    handd(1)
-    xwait2(1)
-    handq(1)
+    ypass(1, "e")
+    xwait(1)
+    hand(1, "q", 2)
+    ywait(1, "c")
+    hand(1, "c")
     halo_wait(1)
     shifts(xs1, (0, 2), 2, 2)
     shifts(xs1, (0, 1, 2), 0, 2)
-    acc[...] = frames[...].astype(F32).reshape(2 * W, C)
-    handwait(1)
-    conv(1, 0, 9)
+    taken(1, "b")
+    conv(1, 0, 5)
+    ywait(1, "e")
+    hand(1, "e")
+    taken(1, "c")
+    conv(1, 1, 6)
+    alltaken(1)
+    conv(1, 3, 8)
+    taken(1, "e")
+    conv(1, 2, 4, 7)
 
     bs[1, 1] = acc[...].astype(BF).reshape(2, W, C)
     send("bu", bs.at[1, 1], rdev(1), bs.at[1, 0], inner_hi)
@@ -417,8 +502,8 @@
         in_specs=[vmem] * 8,
         out_specs=vmem,
         scratch_shapes=[
-            pltpu.VMEM((8, NU, 16, 128), BF),
-            pltpu.VMEM((8, NU, 16, 128), BF),
+            pltpu.VMEM((8, ND[0] + NQ[0], 16, 128), BF),
+            pltpu.VMEM((8, ND[1] + NQ[1], 16, 128), BF),
             pltpu.VMEM((2 * NC, C, 128), BF),
             pltpu.VMEM((2 * NC, C, 128), BF),
             pltpu.VMEM((3, 3, 4, W, C), BF),
@@ -428,8 +513,8 @@
             pltpu.VMEM((2, 2, 2, 2, CO, C), BF),
             pltpu.VMEM((2, 2, 2 * W, CO), F32),
             pltpu.VMEM((4, 2 * W, 128), F32),
-            pltpu.SemaphoreType.DMA((64,)),
-            pltpu.SemaphoreType.DMA((64,)),
+            pltpu.SemaphoreType.DMA((136,)),
+            pltpu.SemaphoreType.DMA((136,)),
         ],
         compiler_params=pltpu.CompilerParams(
             collective_id=0, has_side_effects=True, vmem_limit_bytes=60 << 20

time: 115 us -> 107 us (0.930)
  Pallas kernels: 110 us -> 101 us
    pallas_call x1, Pallas kernels: 110 us -> 101 us  [shards(): pl.pallas_call(kernel, out_shape=jax.ShapeDtypeStruct((2, 2, 2 * W, CO),...]
where the time goes in v2:
time: 107 us; the launch traced here: 106 us
  Pallas kernels  101 us (94%)
  local copies, waits for them, and re-layouts  4.64 us (4%)
    pallas_call x1, Pallas kernels, shards(): pl.pallas_call(kernel, out_shape=jax.ShapeDtypeStruct((2, 2, 2 * W, CO),...  101 us
    pallas_call x1, local copies, waits for them, and re-layouts, shards(): pl.pallas_call(kernel, out_shape=jax.ShapeDtypeStruct((2, 2, 2 * W, CO),...  2.18 us

profile of v2, /device:TPU:10, one launch (start us, length us, event | category | flops | bytes accessed | tf_op | source)
XLA Modules:
  0.0 105.9 jit_solution(15365892740648812891)
XLA Ops:
  0.0 1.2 %reshape.24.gain0 = f32[1,384]{1,0:T(1,128)} reshape(f32[384]{0:T(512)} %param.11) | data formatting | bytes 3072 | tf_op jit(solution)/shard_map/reshape | solution.py:526
  1.2 1.2 %reshape.25.gain1 = f32[1,384]{1,0:T(1,128)} reshape(f32[384]{0:T(512)} %param.12) | data formatting | bytes 3072 | tf_op jit(solution)/shard_map/reshape | solution.py:527
  2.5 101.2 %shard_map.82 = bf16[2,2,320,192]{3,2,1,0:T(8,128)(2,1)} custom-call(bf16[2,160,384]{2,1,0:T(8,128)(2,1)} %bitcast.13, bf16[2,160,384]{2,1,0:T(8,128)(2,1)} %bitcast.14, bf16[2,160,384]{2,1,0:T(8,128)(2,1)} %bitcast.15, f32[1,384]{1,0:T(1,128)} %reshape.24.gain0, f32[1,384]{1,0:T(1,128)} %reshape.25.gain1, bf16[27,12,384]{2,1,0:T(8,128)(2,1)} %bitcast.11, ...), custom_call_target="tpu_custom_call" | custom-call | tf_op jit(solution)/shard_map/pallas_call | solution.py:499
  103.7 2.2 %copy.9 = bf16[2,2,320,192]{2,3,1,0:T(8,128)(2,1)} copy(bf16[2,2,320,192]{3,2,1,0:T(8,128)(2,1)} %shard_map.82) | data formatting | bytes 983040 | tf_op jit(solution)/shard_map/pallas_call | solution.py:499

commit v3 on v2

--- a/solution.py
+++ b/solution.py
@@ -177,24 +177,37 @@
         for n in range(count):
             ws[v][first + n, pl.ds(ybase(0), 96), :] = rows[:, 128 * n : 128 * n + 128]
 
-    def yview(v, g, d, part):
+    def yview(v, g, d, part, core=None):
         lo, n = split(v, g, part)
         lo = lo - chunks[v][g][0]
-        return ws[v].at[pl.ds(base(v, g, c) + lo, n), pl.ds(ybase(d), 96), :]
+        first = base(v, g, c if core is None else core) + lo
+        return ws[v].at[pl.ds(first, n), pl.ds(ybase(d), 96), :]
 
     def ystart(v, g):
         send(("yf1", v, g), yview(v, g, 0, 0), ydev(1))
         send(("yb1", v, g), yview(v, g, 0, 0), ydev(-1))
+        yhand(v, g, 0)
 
     def ypass(v, g):
         recv(("yf1", v, g), yview(v, g, -1, 0))
-        send(("yf2", v, g), yview(v, g, -1, 1), ydev(1))
+        send(("yf2", v, g), yview(v, g, -1, 1), ydev(1), when=z != 0)
         recv(("yb1", v, g), yview(v, g, 1, 0))
-        send(("yb2", v, g), yview(v, g, 1, 2), ydev(-1))
+        send(("yb2", v, g), yview(v, g, 1, 2), ydev(-1), when=z != 7)
+        yhand(v, g, -1)
+        yhand(v, g, 1)
 
     def ywait(v, g):
-        recv(("yf2", v, g), yview(v, g, -2, 1))
-        recv(("yb2", v, g), yview(v, g, 2, 2))
+        recv(("yf2", v, g), yview(v, g, -2, 1), z != 0)
+        send(("ye1", v, g), yview(v, g, -2, 1), zdev(-1), when=z == 1)
+        recv(("yb2", v, g), yview(v, g, 2, 2), z != 7)
+        send(("ye2", v, g), yview(v, g, 2, 2), zdev(1), when=z == 6)
+        recv(("ye1", v, g), yview(v, g, -2, 1), z == 0)
+        recv(("ye2", v, g), yview(v, g, 2, 2), z == 7)
+        yhand(v, g, 2)
+
+    def yhand(v, g, d):
+        if g != "q":
+            send(("h", v, g, d), yview(v, g, d, 0), pair)
 
     def xview(v, d, part):
         lo, n = ((0, 1), (1, NQ[v] - 1))[part - 1]
@@ -218,22 +231,23 @@
         recv(("xf", v, 3), xview(v, -2, 1))
         recv(("xb", v, 3), xview(v, 2, 2))
 
-    def cview(v, g, core, d=0):
-        return ws[v].at[pl.ds(base(v, g, core, d), chunks[v][g][1])]
-
-    def hand(v, g, d=0):
-        send(("c", v, g, d), cview(v, g, c, d), pair)
-
-    def taken(v, g, d=0):
-        recv(("c", v, g, d), cview(v, g, 1 - c, d))
+    def cview(v, core, d):
+        return ws[v].at[pl.ds(qbase(v, core, d), NQ[v])]
+
+    def hand(v, g, d):
+        send(("c", v, g, d), cview(v, c, d), pair)
+
+    def taken(v, g):
+        for d in (0, -1, 1, 2):
+            recv(("h", v, g, d), yview(v, g, d, 0, 1 - c))
 
     def alltaken(v):
         for d in (0, 1, -1, 2):
-            taken(v, "q", d)
+            recv(("c", v, "q", d), cview(v, 1 - c, d))
 
     def normed(v, values):
         scale = lax.rsqrt(jnp.mean(values * values, axis=-1, keepdims=True) + 1e-06)
-        return jax.nn.silu(values * scale * gains[v][...]).astype(BF)
+        return jax.nn.silu(values * scale * gains[v][...].reshape(1, C)).astype(BF)
 
     inner_lo, inner_hi, later, first = r > 0, r < 31, tm < 7, tm == 0
 
@@ -386,13 +400,11 @@
     ystart(1, "q")
     xpass(0, -1)
     ywait(0, "b")
-    hand(0, "b")
     halo_pass(0)
     zwait(1, "b")
     assemble(1, "b")
     ystart(1, "b")
     ywait(0, "c")
-    hand(0, "c")
     xsides(0)
     hand(0, "q", 1)
     hand(0, "q", -1)
@@ -430,7 +442,6 @@
     ypass(1, "c")
     combine()
     ywait(1, "b")
-    hand(1, "b")
     xsides(1)
     hand(1, "q", 1)
     hand(1, "q", -1)
@@ -439,14 +450,12 @@
     xwait(1)
     hand(1, "q", 2)
     ywait(1, "c")
-    hand(1, "c")
     halo_wait(1)
     shifts(xs1, (0, 2), 2, 2)
     shifts(xs1, (0, 1, 2), 0, 2)
     taken(1, "b")
     conv(1, 0, 5)
     ywait(1, "e")
-    hand(1, "e")
     taken(1, "c")
     conv(1, 1, 6)
     alltaken(1)
@@ -513,8 +522,8 @@
             pltpu.VMEM((2, 2, 2, 2, CO, C), BF),
             pltpu.VMEM((2, 2, 2 * W, CO), F32),
             pltpu.VMEM((4, 2 * W, 128), F32),
-            pltpu.SemaphoreType.DMA((136,)),
-            pltpu.SemaphoreType.DMA((136,)),
+            pltpu.SemaphoreType.DMA((176,)),
+            pltpu.SemaphoreType.DMA((176,)),
         ],
         compiler_params=pltpu.CompilerParams(
             collective_id=0, has_side_effects=True, vmem_limit_bytes=60 << 20
@@ -523,8 +532,8 @@
         block(frames),
         block(cache0),
         block(cache1),
-        gain0.reshape(1, C),
-        gain1.reshape(1, C),
+        gain0,
+        gain1,
         flip(first),
         flip(second),
         jnp.swapaxes(upsample, 2, 3),

time: 107 us -> 104 us (0.972)
  local copies, waits for them, and re-layouts: 4.64 us -> 2.18 us
    reshape x2 -> x0, local copies, waits for them, and re-layouts: 2.47 us -> none  [the longest x1 1.24 us: shards(): gain0.reshape(1, C)]
where the time goes in v3:
time: 104 us; the launch traced here: 103 us
  Pallas kernels  101 us (97%)
  local copies, waits for them, and re-layouts  2.18 us (2%)
    pallas_call x1, Pallas kernels, shards(): pl.pallas_call(kernel, out_shape=jax.ShapeDtypeStruct((2, 2, 2 * W, CO),...  101 us
    pallas_call x1, local copies, waits for them, and re-layouts, shards(): pl.pallas_call(kernel, out_shape=jax.ShapeDtypeStruct((2, 2, 2 * W, CO),...  2.18 us

profile of v3, /device:TPU:10, one launch (start us, length us, event | category | flops | bytes accessed | tf_op | source)
XLA Modules:
  0.0 103.0 jit_solution(9965292294961373077)
XLA Ops:
  0.0 100.8 %shard_map.82 = bf16[2,2,320,192]{3,2,1,0:T(8,128)(2,1)} custom-call(bf16[2,160,384]{2,1,0:T(8,128)(2,1)} %bitcast.13, bf16[2,160,384]{2,1,0:T(8,128)(2,1)} %bitcast.14, bf16[2,160,384]{2,1,0:T(8,128)(2,1)} %bitcast.15, f32[384]{0:T(512)} %gain0.1, f32[384]{0:T(512)} %gain1.1, bf16[27,12,384]{2,1,0:T(8,128)(2,1)} %bitcast.11, bf16[27,12,384]{2,1,0:T(8,128)(2,1)} %bitcast.12, ...), custom_call_target="tpu_custom_call" | custom-call | tf_op jit(solution)/shard_map/pallas_call | solution.py:508
  100.8 2.2 %copy.9 = bf16[2,2,320,192]{2,3,1,0:T(8,128)(2,1)} copy(bf16[2,2,320,192]{3,2,1,0:T(8,128)(2,1)} %shard_map.82) | data formatting | bytes 983040 | tf_op jit(solution)/shard_map/pallas_call | solution.py:508

commit v4 on v3

--- a/solution.py
+++ b/solution.py
@@ -389,6 +389,7 @@
     halo_start(0)
     cache_start(0)
     zstart(1, "r")
+    combine()
     ypass(0, "b")
     xpass(0, 1)
     zpass(1, "q")
@@ -400,16 +401,21 @@
     ystart(1, "q")
     xpass(0, -1)
     ywait(0, "b")
-    halo_pass(0)
     zwait(1, "b")
     assemble(1, "b")
     ystart(1, "b")
+    halo_pass(0)
+    zpass(1, "r")
     ywait(0, "c")
     xsides(0)
     hand(0, "q", 1)
     hand(0, "q", -1)
-    zpass(1, "r")
     ypass(1, "q")
+    zwait(1, "r")
+    assemble(1, "c")
+    ystart(1, "c")
+    assemble(1, "e")
+    ystart(1, "e")
     acc[...] = jnp.zeros_like(acc)
     halo_wait(0)
     shifts(xs0, (0, 2), 2, 2)
@@ -418,50 +424,43 @@
     conv(0, 0, 5)
     xwait(0)
     hand(0, "q", 2)
+    ypass(1, "b")
     ywait(1, "q")
     xstart(1)
     hand(1, "q", 0)
     taken(0, "c")
     conv(0, 1, 6)
-    zwait(1, "r")
-    assemble(1, "c")
-    ystart(1, "c")
-    assemble(1, "e")
-    ystart(1, "e")
-    ypass(1, "b")
     alltaken(0)
     conv(0, 2, 3, 4, 7, 8)
     xs1[1, 1, 2:4] = normed(1, acc[...].astype(BF).astype(F32)).reshape(2, W, C)
     halo_row(1)
     halo_start(1)
     cache_start(1)
+    ypass(1, "c")
     xpass(1, 1)
     acc[...] = frames[...].astype(F32).reshape(2 * W, C)
     shifts(xs1, (1,), 2, 2)
+    ypass(1, "e")
     xpass(1, -1)
-    ypass(1, "c")
-    combine()
     ywait(1, "b")
     xsides(1)
     hand(1, "q", 1)
     hand(1, "q", -1)
     halo_pass(1)
-    ypass(1, "e")
+    ywait(1, "c")
+    ywait(1, "e")
     xwait(1)
     hand(1, "q", 2)
-    ywait(1, "c")
     halo_wait(1)
     shifts(xs1, (0, 2), 2, 2)
     shifts(xs1, (0, 1, 2), 0, 2)
     taken(1, "b")
     conv(1, 0, 5)
-    ywait(1, "e")
     taken(1, "c")
     conv(1, 1, 6)
     alltaken(1)
-    conv(1, 3, 8)
     taken(1, "e")
-    conv(1, 2, 4, 7)
+    conv(1, 2, 3, 4, 7, 8)
 
     bs[1, 1] = acc[...].astype(BF).reshape(2, W, C)
     send("bu", bs.at[1, 1], rdev(1), bs.at[1, 0], inner_hi)

time: 104 us -> 106 us (1.019)
  the two profiles are of different devices: /device:TPU:10 before, /device:TPU:32 now
where the time goes in v4:
time: 106 us; the launch traced here: 105 us
  Pallas kernels  103 us (97%)
  local copies, waits for them, and re-layouts  2.18 us (2%)
    pallas_call x1, Pallas kernels, shards(): pl.pallas_call(kernel, out_shape=jax.ShapeDtypeStruct((2, 2, 2 * W, CO),...  103 us
    pallas_call x1, local copies, waits for them, and re-layouts, shards(): pl.pallas_call(kernel, out_shape=jax.ShapeDtypeStruct((2, 2, 2 * W, CO),...  2.18 us

profile of v4, /device:TPU:32, one launch (start us, length us, event | category | flops | bytes accessed | tf_op | source)
XLA Modules:
  0.0 105.5 jit_solution(920741575473866453)
XLA Ops:
  0.0 103.3 %shard_map.82 = bf16[2,2,320,192]{3,2,1,0:T(8,128)(2,1)} custom-call(bf16[2,160,384]{2,1,0:T(8,128)(2,1)} %bitcast.13, bf16[2,160,384]{2,1,0:T(8,128)(2,1)} %bitcast.14, bf16[2,160,384]{2,1,0:T(8,128)(2,1)} %bitcast.15, f32[384]{0:T(512)} %gain0.1, f32[384]{0:T(512)} %gain1.1, bf16[27,12,384]{2,1,0:T(8,128)(2,1)} %bitcast.11, bf16[27,12,384]{2,1,0:T(8,128)(2,1)} %bitcast.12, ...), custom_call_target="tpu_custom_call" | custom-call | tf_op jit(solution)/shard_map/pallas_call | solution.py:507
  103.3 2.2 %copy.9 = bf16[2,2,320,192]{2,3,1,0:T(8,128)(2,1)} copy(bf16[2,2,320,192]{3,2,1,0:T(8,128)(2,1)} %shard_map.82) | data formatting | bytes 983040 | tf_op jit(solution)/shard_map/pallas_call | solution.py:507

commit v5 on v3

--- a/solution.py
+++ b/solution.py
@@ -320,21 +320,34 @@
     def conv(v, *pieces):
         xs, w = xss[v], ws[v]
 
-        def body(n, _):
+        def pick(n):
             ij = jnp.int32(pieces[0])
             for m in range(1, len(pieces)):
                 ij = jnp.where(n == m, pieces[m], ij)
-            i, j = ij // 3, ij % 3
-            low = 9 * ij - jnp.where((ij == 5) | (ij == 6), 4, 0)
-            high = low + jnp.where(ij == 4, 18, 0)
-            lhs = jnp.concatenate(
-                [xs[k, j, pl.ds(i, 2)].reshape(2 * W, C) for k in range(3)], axis=1
+            return ij
+
+        def add(*several):
+            lhs, rhs = [], []
+            for ij in several:
+                i, j = ij // 3, ij % 3
+                low = 9 * ij - jnp.where((ij == 5) | (ij == 6), 4, 0)
+                high = low + jnp.where(ij == 4, 18, 0)
+                lhs += [xs[k, j, pl.ds(i, 2)].reshape(2 * W, C) for k in range(3)]
+                rhs += [w[(low if u < 5 else high) + u] for u in range(9)]
+            acc[...] += lax.dot_general(
+                jnp.concatenate(lhs, axis=1),
+                jnp.concatenate(rhs, axis=1),
+                NT,
+                preferred_element_type=F32,
             )
-            rhs = jnp.concatenate([w[(low if u < 5 else high) + u] for u in range(9)], axis=1)
-            acc[...] += lax.dot_general(lhs, rhs, NT, preferred_element_type=F32)
+
+        def body(n, _):
+            add(pick(2 * n), pick(2 * n + 1))
             return 0
 
-        lax.fori_loop(0, len(pieces), body, 0)
+        lax.fori_loop(0, len(pieces) // 2, body, 0)
+        if len(pieces) % 2:
+            add(jnp.int32(pieces[-1]))
 
     def combine():
         for a in range(2):
@@ -419,8 +432,6 @@
     xwait(0)
     hand(0, "q", 2)
     ywait(1, "q")
-    xstart(1)
-    hand(1, "q", 0)
     taken(0, "c")
     conv(0, 1, 6)
     zwait(1, "r")
@@ -435,11 +446,13 @@
     halo_row(1)
     halo_start(1)
     cache_start(1)
+    xstart(1)
+    hand(1, "q", 0)
+    ypass(1, "c")
     xpass(1, 1)
     acc[...] = frames[...].astype(F32).reshape(2 * W, C)
     shifts(xs1, (1,), 2, 2)
     xpass(1, -1)
-    ypass(1, "c")
     combine()
     ywait(1, "b")
     xsides(1)

time: 104 us -> 107 us (1.029)
  Pallas kernels: 101 us -> 104 us
    pallas_call x1, Pallas kernels: 101 us -> 104 us  [shards(): pl.pallas_call(kernel, out_shape=jax.ShapeDtypeStruct((2, 2, 2 * W, CO),...]
where the time goes in v5:
time: 107 us
  Pallas kernels  104 us (97%)
  local copies, waits for them, and re-layouts  2.18 us (2%)
    pallas_call x1, Pallas kernels, shards(): pl.pallas_call(kernel, out_shape=jax.ShapeDtypeStruct((2, 2, 2 * W, CO),...  104 us
    pallas_call x1, local copies, waits for them, and re-layouts, shards(): pl.pallas_call(kernel, out_shape=jax.ShapeDtypeStruct((2, 2, 2 * W, CO),...  2.18 us

profile of v5, /device:TPU:10, one launch (start us, length us, event | category | flops | bytes accessed | tf_op | source)
XLA Modules:
  0.0 106.6 jit_solution(3318926634987528820)
XLA Ops:
  0.0 104.4 %shard_map.82 = bf16[2,2,320,192]{3,2,1,0:T(8,128)(2,1)} custom-call(bf16[2,160,384]{2,1,0:T(8,128)(2,1)} %bitcast.13, bf16[2,160,384]{2,1,0:T(8,128)(2,1)} %bitcast.14, bf16[2,160,384]{2,1,0:T(8,128)(2,1)} %bitcast.15, f32[384]{0:T(512)} %gain0.1, f32[384]{0:T(512)} %gain1.1, bf16[27,12,384]{2,1,0:T(8,128)(2,1)} %bitcast.11, bf16[27,12,384]{2,1,0:T(8,128)(2,1)} %bitcast.12, ...), custom_call_target="tpu_custom_call" | custom-call | tf_op jit(solution)/shard_map/pallas_call | solution.py:521
  104.5 2.2 %copy.9 = bf16[2,2,320,192]{2,3,1,0:T(8,128)(2,1)} copy(bf16[2,2,320,192]{3,2,1,0:T(8,128)(2,1)} %shard_map.82) | data formatting | bytes 983040 | tf_op jit(solution)/shard_map/pallas_call | solution.py:521

commit v6 on v3

--- a/solution.py
+++ b/solution.py
@@ -11,11 +11,11 @@
 W = 160
 C = 384
 CO = 192
-ND = (21, 25)
-NQ = (5, 4)
+ND = (25, 29)
+NQ = (4, 3)
 NC = 41
 NB = 9
-CUTS = ((12, 0), (9, 7))
+CUTS = ((16, 0), (9, 11))
 TAPS = (((0,), (1, 2)), ((0, 1), (2,)))
 
 
@@ -459,9 +459,9 @@
     taken(1, "c")
     conv(1, 1, 6)
     alltaken(1)
-    conv(1, 3, 8)
+    conv(1, 8)
     taken(1, "e")
-    conv(1, 2, 4, 7)
+    conv(1, 2, 3, 4, 7)
 
     bs[1, 1] = acc[...].astype(BF).reshape(2, W, C)
     send("bu", bs.at[1, 1], rdev(1), bs.at[1, 0], inner_hi)

time: 104 us -> 107 us (1.029); the launches traced: 103 us -> 107 us
  Pallas kernels: 101 us -> 105 us
    pallas_call x1, Pallas kernels: 101 us -> 105 us  [shards(): pl.pallas_call(kernel, out_shape=jax.ShapeDtypeStruct((2, 2, 2 * W, CO),...]
where the time goes in v6:
time: 107 us
  Pallas kernels  105 us (98%)
  local copies, waits for them, and re-layouts  2.18 us (2%)
    pallas_call x1, Pallas kernels, shards(): pl.pallas_call(kernel, out_shape=jax.ShapeDtypeStruct((2, 2, 2 * W, CO),...  105 us
    pallas_call x1, local copies, waits for them, and re-layouts, shards(): pl.pallas_call(kernel, out_shape=jax.ShapeDtypeStruct((2, 2, 2 * W, CO),...  2.18 us

profile of v6, /device:TPU:10, one launch (start us, length us, event | category | flops | bytes accessed | tf_op | source)
XLA Modules:
  0.0 107.1 jit_solution(16018758205565466106)
XLA Ops:
  0.0 104.9 %shard_map.82 = bf16[2,2,320,192]{3,2,1,0:T(8,128)(2,1)} custom-call(bf16[2,160,384]{2,1,0:T(8,128)(2,1)} %bitcast.13, bf16[2,160,384]{2,1,0:T(8,128)(2,1)} %bitcast.14, bf16[2,160,384]{2,1,0:T(8,128)(2,1)} %bitcast.15, f32[384]{0:T(512)} %gain0.1, f32[384]{0:T(512)} %gain1.1, bf16[27,12,384]{2,1,0:T(8,128)(2,1)} %bitcast.11, bf16[27,12,384]{2,1,0:T(8,128)(2,1)} %bitcast.12, ...), custom_call_target="tpu_custom_call" | custom-call | tf_op jit(solution)/shard_map/pallas_call | solution.py:508
  104.9 2.2 %copy.9 = bf16[2,2,320,192]{2,3,1,0:T(8,128)(2,1)} copy(bf16[2,2,320,192]{3,2,1,0:T(8,128)(2,1)} %shard_map.82) | data formatting | bytes 983040 | tf_op jit(solution)/shard_map/pallas_call | solution.py:508
